TPU v7x, 128 devices: a whole 4x4x4 slice. The times are simulated.
128 devices in a mesh: ctx: 32 (over y, x, core), head: 4 (over z).
Axes of the slice: x: 4, y: 4, z: 4, core: 2. Of those that a mesh axis runs over, the one named last changes fastest.
Arguments:
- queries: bfloat16 [16384, 4096], P('ctx', 'head'), may hold values from -5 to 5
- keys: bfloat16 [16384, 512], P('ctx', 'head'), may hold values from -5 to 5
- values: bfloat16 [16384, 512], P('ctx', 'head'), may hold values from -6 to 6
- doc_ids: int32 [16384], replicated, may hold values from 0 to 31, never falling along the last dimension, each value on 1 to 1536 neighbouring positions
- out_weight: bfloat16 [4096, 8192], P(None, 'head'), may hold values from -0.09375 to 0.09375
Outputs:
- layer_out: bfloat16 [16384, 8192], P('ctx', 'head')
Inputs may be any that keep to these rules, and one draw needn't show every extreme that they name: `doc_ids`: every document holds at most 1536 tokens, and one holds exactly that many.
All inputs are finite; a program needn't handle non-finite values.
Results may differ from a plain program's by a relative error of at most 0.0053.
Values may be sent and summed in bfloat16 or wider, within the bound.
No kernel may reach another device: no remote copies, remote signals or barrier semaphores. Data moves between devices by JAX's collectives and lax.ppermute only.
A program may use at most 128 MiB of HBM per device.

v0:
```python
import jax
import jax.numpy as jnp
from jax import lax
from jax.sharding import PartitionSpec as P

HEAD_SIZE = 128
REACH = 3


def from_behind(block, axis, distance):
    devices = range(lax.axis_size(axis))
    route = [(i - distance, i) for i in devices if i - distance in devices]
    return lax.ppermute(block, axis, route)


def attend_window(queries, key_all, value_all, visible):
    rows_here = queries.shape[0]
    kv_heads = key_all.shape[1] // HEAD_SIZE
    group_width = queries.shape[1] // key_all.shape[1]
    local_span = key_all.shape[0]
    query_heads = queries.reshape(rows_here, kv_heads, group_width, HEAD_SIZE)
    key_heads = key_all.reshape(local_span, kv_heads, HEAD_SIZE)
    value_heads = value_all.reshape(local_span, kv_heads, HEAD_SIZE)
    scores = jnp.einsum(
        "qgjd,kgd->gjqk", query_heads, key_heads, preferred_element_type=jnp.float32
    ) * HEAD_SIZE ** (-0.5)
    masked = jnp.where(visible, scores, -jnp.inf)
    row_peak = jnp.max(masked, axis=3, keepdims=True)
    exponent = jnp.where(visible, jnp.exp(scores - row_peak), 0.0)
    row_total = jnp.sum(exponent, axis=3, keepdims=True)
    weights = exponent.astype(jnp.bfloat16)
    mixture = (
        jnp.einsum("gjqk,kgd->gjqd", weights, value_heads, preferred_element_type=jnp.float32)
        / row_total
    )
    return (
        jnp.transpose(mixture, (2, 0, 1, 3))
        .reshape(rows_here, queries.shape[1])
        .astype(jnp.bfloat16)
    )


def shards(queries, keys, values, doc_ids, out_weight):
    rows_here = keys.shape[0]
    shard_index = lax.axis_index("ctx")
    key_parts = []
    value_parts = []
    for offset in range(REACH, 0, -1):
        arrived = from_behind((keys, values), "ctx", offset)
        key_parts.append(arrived[0])
        value_parts.append(arrived[1])
    key_all = jnp.concatenate(key_parts + [keys], 0)
    value_all = jnp.concatenate(value_parts + [values], 0)
    local_span = key_all.shape[0]
    leading_rows = REACH * rows_here
    doc_pad = jnp.concatenate([jnp.full((leading_rows,), -1, jnp.int32), doc_ids], 0)
    first_row = shard_index * rows_here
    key_docs = lax.dynamic_slice_in_dim(doc_pad, first_row, local_span, 0)
    query_docs = lax.dynamic_slice_in_dim(doc_ids, first_row, rows_here, 0)
    key_rel = lax.iota(jnp.int32, local_span)
    query_rel = leading_rows + lax.iota(jnp.int32, rows_here)
    visible = (query_docs[:, None] == key_docs[None, :]) & (key_rel[None, :] <= query_rel[:, None])
    attended = attend_window(queries, key_all, value_all, visible)
    projected = jnp.dot(
        lax.all_gather(attended, "head", axis=1, tiled=True),
        out_weight,
        preferred_element_type=jnp.float32,
    )
    return projected.astype(jnp.bfloat16)


def solution(mesh):
    in_specs = (P("ctx", "head"), P("ctx", "head"), P("ctx", "head"), P(), P(None, "head"))
    out_specs = P("ctx", "head")
    return jax.shard_map(shards, mesh=mesh, in_specs=in_specs, out_specs=out_specs, check_vma=False)
```

profile of v0, /device:TPU:1, one launch (start us, length us, event | category | flops | bytes accessed | tf_op | source)
XLA Modules:
  0.0 145.0 jit_solution(6102187642814633350)
XLA Ops:
  6.5 0.0 copy-start
  6.5 0.0 all-gather.2.cloned.1.call-start
  6.5 1.1 copy.7
  7.6 4.5 %collective-permute-start.5 = (bf16[512,128]{0,1:T(8,128)(2,1)S(1)}, bf16[512,128]{0,1:T(8,128)(2,1)S(1)}, u32[]{:S(2)}, u32[]{:S(2)}) collective-permute-start(bf16[512,128]{0,1:T(8,128)(2,1)S(1)} %copy.7), channel_id=1, source_target_pairs={{0,4},{4,8},{8,12},{12,16},{16,20},{20,24},{24,28},{28,32},{32,36}... | collective-permute-start | bytes 393224 | tf_op jit(solution)/shard_map/ppermute | solution.py:13
  12.2 3.1 %collective-permute-start.4 = (bf16[512,128]{0,1:T(8,128)(2,1)S(1)}, bf16[512,128]{0,1:T(8,128)(2,1)S(1)}, u32[]{:S(2)}, u32[]{:S(2)}) collective-permute-start(bf16[512,128]{0,1:T(8,128)(2,1)S(1)} %copy.7), channel_id=1, source_target_pairs={{0,8},{4,12},{8,16},{12,20},{16,24},{20,28},{24,32},{28,36},{32,40... | collective-permute-start | bytes 393224 | tf_op jit(solution)/shard_map/ppermute | solution.py:13
  15.3 2.8 %collective-permute-start.1 = (bf16[512,128]{1,0:T(8,128)(2,1)}, bf16[512,128]{1,0:T(8,128)(2,1)S(1)}, u32[]{:S(2)}, u32[]{:S(2)}) collective-permute-start(bf16[512,128]{1,0:T(8,128)(2,1)} %param.6), channel_id=1, source_target_pairs={{0,8},{4,12},{8,16},{12,20},{16,24},{20,28},{24,32},{28,36},{32,40... | collective-permute-start | bytes 393224 | tf_op jit(solution)/shard_map/ppermute | solution.py:13
  18.1 4.0 %collective-permute-start = (bf16[512,128]{1,0:T(8,128)(2,1)}, bf16[512,128]{1,0:T(8,128)(2,1)S(1)}, u32[]{:S(2)}, u32[]{:S(2)}) collective-permute-start(bf16[512,128]{1,0:T(8,128)(2,1)} %param.6), channel_id=1, source_target_pairs={{0,12},{4,16},{8,20},{12,24},{16,28},{20,32},{24,36},{28,40},{32,4... | collective-permute-start | bytes 393224 | tf_op jit(solution)/shard_map/ppermute | solution.py:13
  22.1 2.5 %collective-permute-start.2 = (bf16[512,128]{1,0:T(8,128)(2,1)}, bf16[512,128]{1,0:T(8,128)(2,1)S(1)}, u32[]{:S(2)}, u32[]{:S(2)}) collective-permute-start(bf16[512,128]{1,0:T(8,128)(2,1)} %param.6), channel_id=1, source_target_pairs={{0,4},{4,8},{8,12},{12,16},{16,20},{20,24},{24,28},{28,32},{32,36}... | collective-permute-start | bytes 393224 | tf_op jit(solution)/shard_map/ppermute | solution.py:13
  24.7 0.8 dynamic_slice.6
  25.4 0.8 pad_dynamic-slice_fusion
  26.2 0.9 fusion.9
  27.2 0.0 collective-permute-done.1
  27.2 3.5 %collective-permute-start.3 = (bf16[512,128]{0,1:T(8,128)(2,1)S(1)}, bf16[512,128]{0,1:T(8,128)(2,1)S(1)}, u32[]{:S(2)}, u32[]{:S(2)}) collective-permute-start(bf16[512,128]{0,1:T(8,128)(2,1)S(1)} %copy.7), channel_id=1, source_target_pairs={{0,12},{4,16},{8,20},{12,24},{16,28},{20,32},{24,36},{28,40},{32,4... | collective-permute-start | bytes 393224 | tf_op jit(solution)/shard_map/ppermute | solution.py:13
  30.7 0.0 collective-permute-done
  30.7 0.0 collective-permute-done.2
  30.7 0.0 copy-done
  30.7 14.3 %fusion = (f32[8,512]{1,0:T(8,128)S(1)}, f32[2048,512,8]{1,0,2:T(8,128)}) fusion(pred[512,2048]{0,1:T(8,128)(4,1)S(1)} %fusion.9, bf16[512,128]{1,0:T(8,128)(2,1)} %param.6, bf16[512,128]{1,0:T(8,128)(2,1)S(1)} %collective-permute-done.2, bf16[512,128]{1,0:T(8,128)(2,1)S(1)} %collective-permute-done.1, bf16[512,128]{1,0:T(8,128)(2,1)S(1)} %collective-permute-done, ...), kind=kOutput, calls=%fused_computation.2 | convolution fusion | flops 2174742528 | bytes 36192256 | tf_op jit(solution)/shard_map/qgjd,kgd->gjqk/dot_general | solution.py:24
  45.0 14.4 %fusion.3 = f32[8,512]{1,0:T(8,128)S(1)} fusion(f32[2048,512,8]{1,0,2:T(8,128)} %get-tuple-element.6, f32[8,512]{1,0:T(8,128)S(1)} %get-tuple-element.5, pred[512,2048]{0,1:T(8,128)(4,1)S(1)} %fusion.9), kind=kLoop, calls=%fused_computation.5 | loop fusion | flops 33550336 | bytes 34635776 | tf_op jit(solution)/shard_map/reduce_sum | solution.py:30
  59.4 0.0 collective-permute-done.5
  59.4 0.0 collective-permute-done.4
  59.4 0.0 collective-permute-done.3
  59.4 15.5 %divide_convert_fusion = bf16[8,512,128]{1,2,0:T(8,128)(2,1)} fusion(f32[8,512]{1,0:T(8,128)S(1)} %fusion.3, f32[2048,512,8]{1,0,2:T(8,128)} %get-tuple-element.6, f32[8,512]{1,0:T(8,128)S(1)} %get-tuple-element.5, pred[512,2048]{0,1:T(8,128)(4,1)S(1)} %fusion.9, bf16[512,128]{0,1:T(8,128)(2,1)S(1)} %copy.7, ...), kind=kOutput, calls=%fused_computation.13 | convolution fusion | flops 2184183808 | bytes 36208640 | tf_op jit(solution)/shard_map/gjqk,kgd->gjqd/dot_general | solution.py:33
  74.9 0.0 all-gather.2.cloned.1.call-update
  75.0 48.6 %all-gather.2.cloned.1.call-done = bf16[512,4096]{0,1:T(8,128)(2,1)} async-done(((bf16[512,1024]{0,1:T(8,128)(2,1)}), bf16[512,4096]{0,1:T(8,128)(2,1)}) %all-gather.2.cloned.1.call-update) | async-done | bytes 4194320 | tf_op jit(solution)/shard_map/all_gather | solution.py:65
  123.6 14.6 %convolution_convert_fusion = bf16[512,2048]{1,0:T(8,128)(2,1)} fusion(bf16[512,4096]{0,1:T(8,128)(2,1)} %all-gather.2.cloned.1.call-done, bf16[4096,2048]{1,0:T(8,128)(2,1)} %param.9), kind=kOutput, calls=%fused_computation.12 | convolution fusion | flops 8590983168 | bytes 23068672 | tf_op jit(solution)/shard_map/dot_general | solution.py:64
  (1 shorter events, 0.0 us)
Async XLA Ops:
  6.5 24.1 %copy-start = (bf16[512,1024]{1,0:T(8,128)(2,1)S(1)}, bf16[512,1024]{1,0:T(8,128)(2,1)}, u32[]{:S(2)}) copy-start(bf16[512,1024]{1,0:T(8,128)(2,1)} %param.5) | copy-start | bytes 3145732
  6.5 117.1 %all-gather.2.cloned.1.call-start = ((), (), s32[]{:S(2)}) async-start(), calls=%async_computation | async-start | bytes 5242880 | tf_op jit(solution)/shard_map/all_gather | solution.py:65
  7.6 51.8 %collective-permute-start.5 = (bf16[512,128]{0,1:T(8,128)(2,1)S(1)}, bf16[512,128]{0,1:T(8,128)(2,1)S(1)}, u32[]{:S(2)}, u32[]{:S(2)}) collective-permute-start(bf16[512,128]{0,1:T(8,128)(2,1)S(1)} %copy.7), channel_id=1, source_target_pairs={{0,4},{4,8},{8,12},{12,16},{16,20},{20,24},{24,28},{28,32},{32,36}... | collective-permute-start | bytes 393224 | tf_op jit(solution)/shard_map/ppermute | solution.py:13
  12.2 47.3 %collective-permute-start.4 = (bf16[512,128]{0,1:T(8,128)(2,1)S(1)}, bf16[512,128]{0,1:T(8,128)(2,1)S(1)}, u32[]{:S(2)}, u32[]{:S(2)}) collective-permute-start(bf16[512,128]{0,1:T(8,128)(2,1)S(1)} %copy.7), channel_id=1, source_target_pairs={{0,8},{4,12},{8,16},{12,20},{16,24},{20,28},{24,32},{28,36},{32,40... | collective-permute-start | bytes 393224 | tf_op jit(solution)/shard_map/ppermute | solution.py:13
  15.3 11.9 %collective-permute-start.1 = (bf16[512,128]{1,0:T(8,128)(2,1)}, bf16[512,128]{1,0:T(8,128)(2,1)S(1)}, u32[]{:S(2)}, u32[]{:S(2)}) collective-permute-start(bf16[512,128]{1,0:T(8,128)(2,1)} %param.6), channel_id=1, source_target_pairs={{0,8},{4,12},{8,16},{12,20},{16,24},{20,28},{24,32},{28,36},{32,40... | collective-permute-start | bytes 393224 | tf_op jit(solution)/shard_map/ppermute | solution.py:13
  18.1 12.5 %collective-permute-start = (bf16[512,128]{1,0:T(8,128)(2,1)}, bf16[512,128]{1,0:T(8,128)(2,1)S(1)}, u32[]{:S(2)}, u32[]{:S(2)}) collective-permute-start(bf16[512,128]{1,0:T(8,128)(2,1)} %param.6), channel_id=1, source_target_pairs={{0,12},{4,16},{8,20},{12,24},{16,28},{20,32},{24,36},{28,40},{32,4... | collective-permute-start | bytes 393224 | tf_op jit(solution)/shard_map/ppermute | solution.py:13
  22.1 8.5 %collective-permute-start.2 = (bf16[512,128]{1,0:T(8,128)(2,1)}, bf16[512,128]{1,0:T(8,128)(2,1)S(1)}, u32[]{:S(2)}, u32[]{:S(2)}) collective-permute-start(bf16[512,128]{1,0:T(8,128)(2,1)} %param.6), channel_id=1, source_target_pairs={{0,4},{4,8},{8,12},{12,16},{16,20},{20,24},{24,28},{28,32},{32,36}... | collective-permute-start | bytes 393224 | tf_op jit(solution)/shard_map/ppermute | solution.py:13
  27.2 32.3 %collective-permute-start.3 = (bf16[512,128]{0,1:T(8,128)(2,1)S(1)}, bf16[512,128]{0,1:T(8,128)(2,1)S(1)}, u32[]{:S(2)}, u32[]{:S(2)}) collective-permute-start(bf16[512,128]{0,1:T(8,128)(2,1)S(1)} %copy.7), channel_id=1, source_target_pairs={{0,12},{4,16},{8,20},{12,24},{16,28},{20,32},{24,36},{28,40},{32,4... | collective-permute-start | bytes 393224 | tf_op jit(solution)/shard_map/ppermute | solution.py:13
Sparse Core Ops, SparseCore 0:
  75.1 48.4 all-gather.1
where the time goes:
time: 145 us
  waiting for transfers between devices  48.7 us (34%)
  matrix products  44.4 us (31%)
  starting transfers between devices  20.4 us (14%)
  other arithmetic  15.3 us (11%)
  between operations  13.5 us (9%)
  local copies, waits for them, and re-layouts  2.64 us (2%)
    all_gather x1, waiting for transfers between devices, shards(): lax.all_gather(attended, 'head', axis=1, tiled=True)  48.6 us
    ppermute x6, starting transfers between devices, from_behind(): return lax.ppermute(block, axis, route)  20.4 us
    dot_general x1, matrix products, attend_window(): jnp.einsum('gjqk,kgd->gjqd', weights, value_heads, preferred_element_type...  15.5 us
    dot_general x1, matrix products, shards(): jnp.dot(lax.all_gather(attended, 'head', axis=1, tiled=True), out_weight,...  14.6 us
    reduce_sum x1, other arithmetic, attend_window(): row_total = jnp.sum(exponent, axis=3, keepdims=True)  14.4 us
    dot_general x1, matrix products, attend_window(): jnp.einsum('qgjd,kgd->gjqk', query_heads, key_heads, preferred_element_ty...  14.3 us
  transfers between devices with their start and end apart: 7, of which 1 were waited for; matrix products, arithmetic and copies ran while one was open for 22% of the time, Pallas kernels for 0%

commit v1 on v0

--- a/solution.py
+++ b/solution.py
@@ -5,6 +5,27 @@
 
 HEAD_SIZE = 128
 REACH = 3
+
+
+def gather_around(x, axis, dim):
+    peers, position, rows = (lax.axis_size(axis), lax.axis_index(axis), x.shape[dim])
+    right = [(i, (i + 1) % peers) for i in range(peers)]
+    behind = [(i, (i - 1) % peers) for i in range(peers)]
+    filled = jnp.zeros((*x.shape[:dim], peers * rows, *x.shape[dim + 1 :]), x.dtype)
+    filled = lax.dynamic_update_slice_in_dim(filled, x, position * rows, axis=dim)
+    from_left = from_right = x
+    half = peers // 2
+    for step in range(1, half + 1):
+        from_left = lax.ppermute(from_left, axis, right)
+        filled = lax.dynamic_update_slice_in_dim(
+            filled, from_left, (position - step) % peers * rows, axis=dim
+        )
+        if step < peers - half:
+            from_right = lax.ppermute(from_right, axis, behind)
+            filled = lax.dynamic_update_slice_in_dim(
+                filled, from_right, (position + step) % peers * rows, axis=dim
+            )
+    return filled
 
 
 def from_behind(block, axis, distance):
@@ -62,9 +83,7 @@
     visible = (query_docs[:, None] == key_docs[None, :]) & (key_rel[None, :] <= query_rel[:, None])
     attended = attend_window(queries, key_all, value_all, visible)
     projected = jnp.dot(
-        lax.all_gather(attended, "head", axis=1, tiled=True),
-        out_weight,
-        preferred_element_type=jnp.float32,
+        gather_around(attended, "head", 1), out_weight, preferred_element_type=jnp.float32
     )
     return projected.astype(jnp.bfloat16)
 

time: 145 us -> 136 us (0.938)
  between operations: 13.5 us -> 0.19 us
  starting transfers between devices: 20.4 us -> 24.7 us
  local copies, waits for them, and re-layouts: 2.64 us -> 5.71 us
  waiting for transfers between devices: 48.7 us -> 46.9 us
  matrix products: 44.4 us -> 42.6 us
    all_gather x1 -> x0, waiting for transfers between devices: 48.6 us -> none  [shards(): lax.all_gather(attended, 'head', axis=1, tiled=True)]
    ppermute x0 -> x3, waiting for transfers between devices: none -> 46.9 us  [the longest x2 46.9 us: gather_around(): from_left = lax.ppermute(from_left, axis, right)]
    ppermute x0 -> x3, starting transfers between devices: none -> 3.92 us  [the longest x1 2.2 us: gather_around(): from_right = lax.ppermute(from_right, axis, behind)]
    dynamic_update_slice x0 -> x4, local copies, waits for them, and re-layouts: none -> 2.87 us  [the longest x2 1.43 us: gather_around(): lax.dynamic_update_slice_in_dim(filled, from_left, (position - step) % pe...]
  transfers between devices with their start and end apart: 7 -> 9, of which waited for: 1 -> 2; matrix products, arithmetic and copies ran while one was open for 22% -> 25% of each run, Pallas kernels for 0% -> 0%
where the time goes in v1:
time: 136 us; the launch traced here: 135 us
  waiting for transfers between devices  46.9 us (34%)
  matrix products  42.6 us (31%)
  starting transfers between devices  24.7 us (18%)
  other arithmetic  15.3 us (11%)
  local copies, waits for them, and re-layouts  5.71 us (4%)
    ppermute x2, waiting for transfers between devices, gather_around(): from_left = lax.ppermute(from_left, axis, right)  46.9 us
    ppermute x6, starting transfers between devices, from_behind(): return lax.ppermute(block, axis, route)  20.8 us
    dot_general x1, matrix products, attend_window(): jnp.einsum('gjqk,kgd->gjqd', weights, value_heads, preferred_element_type...  14.5 us
    reduce_sum x1, other arithmetic, attend_window(): row_total = jnp.sum(exponent, axis=3, keepdims=True)  14.4 us
    dot_general x1, matrix products, attend_window(): jnp.einsum('qgjd,kgd->gjqk', query_heads, key_heads, preferred_element_ty...  14.3 us
    dot_general x1, matrix products, shards(): jnp.dot(gather_around(attended, 'head', 1), out_weight, preferred_element...  13.7 us
  transfers between devices with their start and end apart: 9, of which 2 were waited for; matrix products, arithmetic and copies ran while one was open for 25% of the time, Pallas kernels for 0%

profile of v1, /device:TPU:1, one launch (start us, length us, event | category | flops | bytes accessed | tf_op | source)
XLA Modules:
  0.0 135.5 jit_solution(9290688750060057690)
XLA Ops:
  0.0 0.0 copy-start
  0.0 6.2 %collective-permute-start = (bf16[512,128]{1,0:T(8,128)(2,1)}, bf16[512,128]{1,0:T(8,128)(2,1)S(1)}, u32[]{:S(2)}, u32[]{:S(2)}) collective-permute-start(bf16[512,128]{1,0:T(8,128)(2,1)} %param.6), channel_id=1, source_target_pairs={{0,12},{4,16},{8,20},{12,24},{16,28},{20,32},{24,36},{28,40},{32,4... | collective-permute-start | bytes 393224 | tf_op jit(solution)/shard_map/ppermute | solution.py:34
  6.2 2.2 %collective-permute-start.1 = (bf16[512,128]{1,0:T(8,128)(2,1)}, bf16[512,128]{1,0:T(8,128)(2,1)S(1)}, u32[]{:S(2)}, u32[]{:S(2)}) collective-permute-start(bf16[512,128]{1,0:T(8,128)(2,1)} %param.6), channel_id=1, source_target_pairs={{0,8},{4,12},{8,16},{12,20},{16,24},{20,28},{24,32},{28,36},{32,40... | collective-permute-start | bytes 393224 | tf_op jit(solution)/shard_map/ppermute | solution.py:34
  8.4 2.2 %collective-permute-start.2 = (bf16[512,128]{1,0:T(8,128)(2,1)}, bf16[512,128]{1,0:T(8,128)(2,1)S(1)}, u32[]{:S(2)}, u32[]{:S(2)}) collective-permute-start(bf16[512,128]{1,0:T(8,128)(2,1)} %param.6), channel_id=1, source_target_pairs={{0,4},{4,8},{8,12},{12,16},{16,20},{20,24},{24,28},{28,32},{32,36}... | collective-permute-start | bytes 393224 | tf_op jit(solution)/shard_map/ppermute | solution.py:34
  10.6 1.0 copy.7
  11.6 4.8 %collective-permute-start.3 = (bf16[512,128]{0,1:T(8,128)(2,1)S(1)}, bf16[512,128]{0,1:T(8,128)(2,1)S(1)}, u32[]{:S(2)}, u32[]{:S(2)}) collective-permute-start(bf16[512,128]{0,1:T(8,128)(2,1)S(1)} %copy.7), channel_id=1, source_target_pairs={{0,12},{4,16},{8,20},{12,24},{16,28},{20,32},{24,36},{28,40},{32,4... | collective-permute-start | bytes 393224 | tf_op jit(solution)/shard_map/ppermute | solution.py:34
  16.4 3.1 %collective-permute-start.4 = (bf16[512,128]{0,1:T(8,128)(2,1)S(1)}, bf16[512,128]{0,1:T(8,128)(2,1)S(1)}, u32[]{:S(2)}, u32[]{:S(2)}) collective-permute-start(bf16[512,128]{0,1:T(8,128)(2,1)S(1)} %copy.7), channel_id=1, source_target_pairs={{0,8},{4,12},{8,16},{12,20},{16,24},{20,28},{24,32},{28,36},{32,40... | collective-permute-start | bytes 393224 | tf_op jit(solution)/shard_map/ppermute | solution.py:34
  19.5 0.8 pad_dynamic-slice_fusion
  20.3 0.8 dynamic_slice.6
  21.1 0.9 fusion.9
  22.0 0.0 collective-permute-done
  22.1 2.4 %collective-permute-start.5 = (bf16[512,128]{0,1:T(8,128)(2,1)S(1)}, bf16[512,128]{0,1:T(8,128)(2,1)S(1)}, u32[]{:S(2)}, u32[]{:S(2)}) collective-permute-start(bf16[512,128]{0,1:T(8,128)(2,1)S(1)} %copy.7), channel_id=1, source_target_pairs={{0,4},{4,8},{8,12},{12,16},{16,20},{20,24},{24,28},{28,32},{32,36}... | collective-permute-start | bytes 393224 | tf_op jit(solution)/shard_map/ppermute | solution.py:34
  24.4 0.0 collective-permute-done.1
  24.4 0.0 collective-permute-done.2
  24.4 0.0 copy-done
  24.5 14.3 %fusion = (f32[8,512]{1,0:T(8,128)S(1)}, f32[2048,512,8]{1,0,2:T(8,128)}) fusion(pred[512,2048]{0,1:T(8,128)(4,1)S(1)} %fusion.9, bf16[512,128]{1,0:T(8,128)(2,1)} %param.6, bf16[512,128]{1,0:T(8,128)(2,1)S(1)} %collective-permute-done.2, bf16[512,128]{1,0:T(8,128)(2,1)S(1)} %collective-permute-done.1, bf16[512,128]{1,0:T(8,128)(2,1)S(1)} %collective-permute-done, ...), kind=kOutput, calls=%fused_computation.2 | convolution fusion | flops 2174742528 | bytes 36192256 | tf_op jit(solution)/shard_map/qgjd,kgd->gjqk/dot_general | solution.py:45
  38.8 14.4 %fusion.3 = f32[8,512]{1,0:T(8,128)S(1)} fusion(f32[2048,512,8]{1,0,2:T(8,128)} %get-tuple-element.6, f32[8,512]{1,0:T(8,128)S(1)} %get-tuple-element.5, pred[512,2048]{0,1:T(8,128)(4,1)S(1)} %fusion.9), kind=kLoop, calls=%fused_computation.5 | loop fusion | flops 33550336 | bytes 34635776 | tf_op jit(solution)/shard_map/reduce_sum | solution.py:51
  53.2 0.0 collective-permute-done.3
  53.2 0.0 collective-permute-done.4
  53.2 0.0 collective-permute-done.5
  53.2 14.5 %divide_convert_fusion = bf16[8,512,128]{1,2,0:T(8,128)(2,1)S(1)} fusion(f32[8,512]{1,0:T(8,128)S(1)} %fusion.3, f32[2048,512,8]{1,0,2:T(8,128)} %get-tuple-element.6, f32[8,512]{1,0:T(8,128)S(1)} %get-tuple-element.5, pred[512,2048]{0,1:T(8,128)(4,1)S(1)} %fusion.9, bf16[512,128]{0,1:T(8,128)(2,1)S(1)} %copy.7, ...), kind=kOutput, calls=%fused_computation.13 | convolution fusion | flops 2184183808 | bytes 36208640 | tf_op jit(solution)/shard_map/gjqk,kgd->gjqd/dot_general | solution.py:54
  67.7 1.7 %collective-permute-start.6 = (bf16[512,1024]{0,1:T(8,128)(2,1)S(1)}, bf16[512,1024]{0,1:T(8,128)(2,1)S(1)}, u32[]{:S(2)}, u32[]{:S(2)}) collective-permute-start(bf16[512,1024]{0,1:T(8,128)(2,1)S(1)} %bitcast.49), channel_id=1, source_target_pairs={{0,1},{1,2},{2,3},{3,0},{4,5},{5,6},{6,7},{7,4},{8,9},{9,10},{10,1... | collective-permute-start | bytes 3145736 | tf_op jit(solution)/shard_map/ppermute | solution.py:19
  69.4 2.2 %collective-permute-start.7 = (bf16[512,1024]{0,1:T(8,128)(2,1)S(1)}, bf16[512,1024]{0,1:T(8,128)(2,1)}, u32[]{:S(2)}, u32[]{:S(2)}) collective-permute-start(bf16[512,1024]{0,1:T(8,128)(2,1)S(1)} %bitcast.50), channel_id=1, source_target_pairs={{0,3},{1,0},{2,1},{3,2},{4,7},{5,4},{6,5},{7,6},{8,11},{9,8},{10,9... | collective-permute-start | bytes 3145736 | tf_op jit(solution)/shard_map/ppermute | solution.py:24
  71.6 23.4 %collective-permute-done.6 = bf16[512,1024]{0,1:T(8,128)(2,1)S(1)} collective-permute-done((bf16[512,1024]{0,1:T(8,128)(2,1)S(1)}, bf16[512,1024]{0,1:T(8,128)(2,1)S(1)}, u32[]{:S(2)}, u32[]{:S(2)}) %collective-permute-start.6) | collective-permute-done | bytes 1048608 | tf_op jit(solution)/shard_map/ppermute | solution.py:19
  95.0 0.0 collective-permute-start.8
  95.0 0.3 broadcast_in_dim.22
  95.3 0.1 constant_dynamic-update-slice_fusion.3
  95.4 0.1 constant_dynamic-update-slice_fusion.2
  95.5 0.0 collective-permute-done.7
  95.5 1.3 constant_dynamic-update-slice_fusion.1
  96.9 23.5 %collective-permute-done.8 = bf16[512,1024]{0,1:T(8,128)(2,1)} collective-permute-done((bf16[512,1024]{0,1:T(8,128)(2,1)S(1)}, bf16[512,1024]{0,1:T(8,128)(2,1)}, u32[]{:S(2)}, u32[]{:S(2)}) %collective-permute-start.8) | collective-permute-done | bytes 1048608 | tf_op jit(solution)/shard_map/ppermute | solution.py:19
  120.4 1.3 constant_dynamic-update-slice_fusion
  121.7 13.7 %convolution_convert_fusion = bf16[512,2048]{1,0:T(8,128)(2,1)} fusion(bf16[512,4096]{0,1:T(8,128)(2,1)S(1)} %constant_dynamic-update-slice_fusion, bf16[4096,2048]{1,0:T(8,128)(2,1)} %param.9), kind=kOutput, calls=%fused_computation.12 | convolution fusion | flops 8590983168 | bytes 23068672 | tf_op jit(solution)/shard_map/dot_general | solution.py:85
  (1 shorter events, 0.0 us)
Async XLA Ops:
  0.0 24.4 %copy-start = (bf16[512,1024]{1,0:T(8,128)(2,1)S(1)}, bf16[512,1024]{1,0:T(8,128)(2,1)}, u32[]{:S(2)}) copy-start(bf16[512,1024]{1,0:T(8,128)(2,1)} %param.5) | copy-start | bytes 3145732
  0.0 22.0 %collective-permute-start = (bf16[512,128]{1,0:T(8,128)(2,1)}, bf16[512,128]{1,0:T(8,128)(2,1)S(1)}, u32[]{:S(2)}, u32[]{:S(2)}) collective-permute-start(bf16[512,128]{1,0:T(8,128)(2,1)} %param.6), channel_id=1, source_target_pairs={{0,12},{4,16},{8,20},{12,24},{16,28},{20,32},{24,36},{28,40},{32,4... | collective-permute-start | bytes 393224 | tf_op jit(solution)/shard_map/ppermute | solution.py:34
  6.2 18.3 %collective-permute-start.1 = (bf16[512,128]{1,0:T(8,128)(2,1)}, bf16[512,128]{1,0:T(8,128)(2,1)S(1)}, u32[]{:S(2)}, u32[]{:S(2)}) collective-permute-start(bf16[512,128]{1,0:T(8,128)(2,1)} %param.6), channel_id=1, source_target_pairs={{0,8},{4,12},{8,16},{12,20},{16,24},{20,28},{24,32},{28,36},{32,40... | collective-permute-start | bytes 393224 | tf_op jit(solution)/shard_map/ppermute | solution.py:34
  8.4 16.0 %collective-permute-start.2 = (bf16[512,128]{1,0:T(8,128)(2,1)}, bf16[512,128]{1,0:T(8,128)(2,1)S(1)}, u32[]{:S(2)}, u32[]{:S(2)}) collective-permute-start(bf16[512,128]{1,0:T(8,128)(2,1)} %param.6), channel_id=1, source_target_pairs={{0,4},{4,8},{8,12},{12,16},{16,20},{20,24},{24,28},{28,32},{32,36}... | collective-permute-start | bytes 393224 | tf_op jit(solution)/shard_map/ppermute | solution.py:34
  11.6 41.5 %collective-permute-start.3 = (bf16[512,128]{0,1:T(8,128)(2,1)S(1)}, bf16[512,128]{0,1:T(8,128)(2,1)S(1)}, u32[]{:S(2)}, u32[]{:S(2)}) collective-permute-start(bf16[512,128]{0,1:T(8,128)(2,1)S(1)} %copy.7), channel_id=1, source_target_pairs={{0,12},{4,16},{8,20},{12,24},{16,28},{20,32},{24,36},{28,40},{32,4... | collective-permute-start | bytes 393224 | tf_op jit(solution)/shard_map/ppermute | solution.py:34
  16.4 36.8 %collective-permute-start.4 = (bf16[512,128]{0,1:T(8,128)(2,1)S(1)}, bf16[512,128]{0,1:T(8,128)(2,1)S(1)}, u32[]{:S(2)}, u32[]{:S(2)}) collective-permute-start(bf16[512,128]{0,1:T(8,128)(2,1)S(1)} %copy.7), channel_id=1, source_target_pairs={{0,8},{4,12},{8,16},{12,20},{16,24},{20,28},{24,32},{28,36},{32,40... | collective-permute-start | bytes 393224 | tf_op jit(solution)/shard_map/ppermute | solution.py:34
  22.1 31.1 %collective-permute-start.5 = (bf16[512,128]{0,1:T(8,128)(2,1)S(1)}, bf16[512,128]{0,1:T(8,128)(2,1)S(1)}, u32[]{:S(2)}, u32[]{:S(2)}) collective-permute-start(bf16[512,128]{0,1:T(8,128)(2,1)S(1)} %copy.7), channel_id=1, source_target_pairs={{0,4},{4,8},{8,12},{12,16},{16,20},{20,24},{24,28},{28,32},{32,36}... | collective-permute-start | bytes 393224 | tf_op jit(solution)/shard_map/ppermute | solution.py:34
  67.7 27.3 %collective-permute-start.6 = (bf16[512,1024]{0,1:T(8,128)(2,1)S(1)}, bf16[512,1024]{0,1:T(8,128)(2,1)S(1)}, u32[]{:S(2)}, u32[]{:S(2)}) collective-permute-start(bf16[512,1024]{0,1:T(8,128)(2,1)S(1)} %bitcast.49), channel_id=1, source_target_pairs={{0,1},{1,2},{2,3},{3,0},{4,5},{5,6},{6,7},{7,4},{8,9},{9,10},{10,1... | collective-permute-start | bytes 3145736 | tf_op jit(solution)/shard_map/ppermute | solution.py:19
  69.4 26.1 %collective-permute-start.7 = (bf16[512,1024]{0,1:T(8,128)(2,1)S(1)}, bf16[512,1024]{0,1:T(8,128)(2,1)}, u32[]{:S(2)}, u32[]{:S(2)}) collective-permute-start(bf16[512,1024]{0,1:T(8,128)(2,1)S(1)} %bitcast.50), channel_id=1, source_target_pairs={{0,3},{1,0},{2,1},{3,2},{4,7},{5,4},{6,5},{7,6},{8,11},{9,8},{10,9... | collective-permute-start | bytes 3145736 | tf_op jit(solution)/shard_map/ppermute | solution.py:24
  95.0 25.4 %collective-permute-start.8 = (bf16[512,1024]{0,1:T(8,128)(2,1)S(1)}, bf16[512,1024]{0,1:T(8,128)(2,1)}, u32[]{:S(2)}, u32[]{:S(2)}) collective-permute-start(bf16[512,1024]{0,1:T(8,128)(2,1)S(1)} %collective-permute-done.6), channel_id=1, source_target_pairs={{0,1},{1,2},{2,3},{3,0},{4,5},{5,6},{6,7},{7,4},{8,9},{9,10},{10,1... | collective-permute-start | bytes 3145736 | tf_op jit(solution)/shard_map/ppermute | solution.py:19
